TPU v7x, 32 devices: a whole 2x2x4 slice. The times are simulated.
32 devices in a mesh: row: 2 (over core), sec: 4 (over y, x), span: 4 (over z).
Axes of the slice: x: 2, y: 2, z: 4, core: 2. Of those that a mesh axis runs over, the one named last changes fastest.
Arguments:
- state: float32 [2, 9, 7, 4, 16, 512], P('row', None, None, None, 'span', 'sec'), may hold values from -6 to 6
- viscosity: float32 [2, 4, 16, 512], P('row', None, 'span', 'sec'), may hold values from 0.1 to 1
- jacobian: float32 [2, 7, 7], P('row'), may hold values from -2 to 2
- frequency: float32 [2], P('row'), may hold values from 0.5 to 2
- offsets: int32 [9], replicated, may hold values from 0 to 511
Outputs:
- updated: float32 [2, 9, 7, 4, 16, 512], P('row', None, None, None, 'span', 'sec')
All inputs are finite; a program needn't handle non-finite values.
Results may differ from a plain program's by a relative error of at most 0.0001.
Values sent between devices are 32-bit elements; how exact they have to be, the bound alone decides.
No kernel may reach another device: no remote copies, remote signals or barrier semaphores. Data moves between devices by JAX's collectives and lax.ppermute only.
A program may use at most 192 MiB of HBM per device.

v0:
```python
import math

import jax
import jax.numpy as jnp
from jax import lax
from jax.sharding import PartitionSpec as P


def from_partner(block, axis, distance):
    count = lax.axis_size(axis)
    route = []
    for low in range(count):
        high = low | 1 << distance
        if high != low and high < count:
            route += [(low, high), (high, low)]
    return lax.ppermute(block, axis, route)


def extended(block, sides, width, periodic):
    for axis, dim in sides:
        count = lax.axis_size(axis)
        forward = [(i, i + 1) for i in range(count - 1)]
        if periodic:
            forward.append((count - 1, 0))
        backward = [(target, source) for source, target in forward]
        low = lax.ppermute(
            lax.slice_in_dim(block, block.shape[dim] - width, None, axis=dim), axis, forward
        )
        high = lax.ppermute(lax.slice_in_dim(block, 0, width, axis=dim), axis, backward)
        block = jnp.concatenate([low, block, high], axis=dim)
    return block


def spectral_matrix(count):
    index = jnp.arange(count)
    offset = index[:, None] - index[None, :]
    parity = jnp.where(jnp.abs(offset) % 2 == 0, 1.0, -1.0).astype(jnp.float32)
    angle = math.pi / count * offset.astype(jnp.float32)
    safe_sin = jnp.where(offset == 0, jnp.float32(1.0), jnp.sin(angle))
    return jnp.where(offset == 0, jnp.float32(0.0), 0.5 * parity / safe_sin)


def on_device(state, viscosity, jacobian, frequency, offsets):
    flow_field_values = state[0]
    coeff = viscosity[0]
    jac_row = jacobian[0]
    omega = frequency[0]
    cells = flow_field_values.shape[-1]
    sectors = lax.axis_size("sec")
    annulus_cells = cells * sectors
    row_index = lax.axis_index("row")
    sec_index = lax.axis_index("sec")
    shift = jnp.where(row_index == 0, offsets, (annulus_cells - offsets) % annulus_cells)
    strip = flow_field_values[:, :, -1]
    other = from_partner(strip, "row", 0)
    whole = lax.all_gather(other, "sec", axis=3, tiled=True)
    local_cells = jnp.arange(cells, dtype=jnp.int32)
    source_index = (sec_index * cells + local_cells[None, :] - shift[:, None]) % annulus_cells
    ghost = jax.vmap(lambda block, where: jnp.take(block, where, axis=2))(whole, source_index)
    periodic_wrapped_state = extended(flow_field_values, (("sec", 4),), 1, True)
    plus_theta = periodic_wrapped_state[..., 2:]
    minus_theta = periodic_wrapped_state[..., :-2]
    slab_split_state = extended(flow_field_values, (("span", 3),), 1, False)
    upper_spanwise_neighbour = slab_split_state[:, :, :, 2:]
    lower_spanwise_neighbour = slab_split_state[:, :, :, :-2]
    plus_axial = jnp.concatenate([flow_field_values[:, :, 1:], ghost[:, :, None]], axis=2)
    minus_axial = jnp.concatenate(
        [jnp.zeros_like(flow_field_values[:, :, :1]), flow_field_values[:, :, :-1]], axis=2
    )
    deriv = spectral_matrix(flow_field_values.shape[0])
    timeterm = jnp.einsum(
        "tu,ufasc->tfasc", deriv, flow_field_values, precision=lax.Precision.HIGHEST
    )
    convect = jnp.einsum(
        "fg,tgasc->tfasc", jac_row, plus_theta - minus_theta, precision=lax.Precision.HIGHEST
    )
    residual = (
        -omega * timeterm
        - 0.5 * convect
        + coeff * (plus_theta + minus_theta - 2.0 * flow_field_values)
        + coeff * (upper_spanwise_neighbour + lower_spanwise_neighbour - 2.0 * flow_field_values)
        + (plus_axial + minus_axial - 2.0 * flow_field_values)
    )
    return (flow_field_values + 0.1 * residual)[None]


def solution(mesh):
    return jax.shard_map(
        on_device,
        mesh=mesh,
        in_specs=(
            P("row", None, None, None, "span", "sec"),
            P("row", None, "span", "sec"),
            P("row", None, None),
            P("row"),
            P(),
        ),
        out_specs=P("row", None, None, None, "span", "sec"),
        check_vma=False,
    )
```

profile of v0, /device:TPU:0, one launch (start us, length us, event | category | flops | bytes accessed | tf_op | source)
XLA Modules:
  0.0 75.3 jit_solution(5151350214854832854)
XLA Ops:
  0.0 1.2 %copy.40 = f32[1,9,7,4,4,128]{5,1,4,3,2,0:T(8,128)S(1)} copy(f32[1,9,7,4,4,128]{5,4,3,2,1,0:T(4,128)} %param.5) | data formatting | bytes 1032192 | tf_op args[0]
  1.2 0.8 %fusion.59 = (f32[9,7,4,1,128]{4,0,3,2,1:T(8,128)}, f32[9,7,4,1,128]{4,0,3,2,1:T(8,128)}) fusion(f32[9,7,4,4,128]{4,0,3,2,1:T(8,128)S(1)} %bitcast.29), kind=kLoop, calls=%fused_computation.91 | loop fusion | bytes 516096 | tf_op jit(solution)/shard_map/slice | solution.py:29
  2.1 5.6 %collective-permute-start.3 = (f32[9,7,4,1,128]{4,0,3,2,1:T(8,128)}, f32[9,7,4,1,128]{4,0,3,2,1:T(8,128)}, u32[]{:S(2)}, u32[]{:S(2)}) collective-permute-start(f32[9,7,4,1,128]{4,0,3,2,1:T(8,128)} %get-tuple-element.10), channel_id=1, source_target_pairs={{0,1},{1,2},{2,3},{4,5},{5,6},{6,7},{8,9},{9,10},{10,11},{12,13},{... | collective-permute-start | bytes 387080 | tf_op jit(solution)/shard_map/ppermute | solution.py:26
  7.7 1.3 %collective-permute-start.2 = (f32[9,7,4,1,128]{4,0,3,2,1:T(8,128)}, f32[9,7,4,1,128]{4,0,3,2,1:T(8,128)}, u32[]{:S(2)}, u32[]{:S(2)}) collective-permute-start(f32[9,7,4,1,128]{4,0,3,2,1:T(8,128)} %get-tuple-element.9), channel_id=1, source_target_pairs={{1,0},{2,1},{3,2},{5,4},{6,5},{7,6},{9,8},{10,9},{11,10},{13,12},{... | collective-permute-start | bytes 387080 | tf_op jit(solution)/shard_map/ppermute | solution.py:29
  9.0 0.7 slice_bitcast_fusion
  9.7 0.0 collective-permute-start.4
  9.7 0.3 fusion.58
  10.0 0.8 %copy.17 = f32[9,7,4,4,1]{0,3,4,2,1:T(4,128)S(1)} copy(f32[9,7,4,4,1]{4,0,3,2,1:T(8,128)S(1)} %get-tuple-element.8) | data formatting | bytes 8064 | tf_op jit(solution)/shard_map/slice | solution.py:29
  10.8 2.5 %collective-permute-start = (f32[9,7,4,4,1]{0,3,4,2,1:T(4,128)S(1)}, f32[9,7,4,4,1]{0,3,4,2,1:T(4,128)S(1)}, u32[]{:S(2)}, u32[]{:S(2)}) collective-permute-start(f32[9,7,4,4,1]{0,3,4,2,1:T(4,128)S(1)} %copy.17), channel_id=1, source_target_pairs={{4,0},{8,4},{12,8},{0,12},{5,1},{9,5},{13,9},{1,13},{6,2},{10,6},{... | collective-permute-start | bytes 12104 | tf_op jit(solution)/shard_map/ppermute | solution.py:29
  13.3 0.8 %copy.19 = f32[9,7,4,4,1]{0,3,4,2,1:T(4,128)S(1)} copy(f32[9,7,4,4,1]{4,0,3,2,1:T(8,128)S(1)} %get-tuple-element.7) | data formatting | bytes 8064 | tf_op jit(solution)/shard_map/slice | solution.py:27
  14.0 0.0 collective-permute-start.1
  14.1 1.1 %fusion.57 = (f32[9,7,3,4,128]{4,0,3,2,1:T(8,128)S(1)}, f32[9,7,3,4,128]{4,0,3,2,1:T(8,128)}) fusion(f32[9,7,4,4,128]{4,0,3,2,1:T(8,128)S(1)} %bitcast.32), kind=kLoop, calls=%fused_computation.89 | loop fusion | bytes 1548288 | tf_op jit(solution)/shard_map/slice | solution.py:68
  15.2 0.7 broadcast_select_fusion
  15.8 0.1 fusion.22
  15.9 0.7 compare_and_fusion
  17.2 0.0 collective-permute-done
  17.3 0.8 %copy.18 = f32[9,7,4,4,1]{4,0,3,2,1:T(8,128)S(1)} copy(f32[9,7,4,4,1]{0,3,4,2,1:T(4,128)S(1)} %collective-permute-done) | data formatting | bytes 8064 | tf_op jit(solution)/shard_map/ppermute | solution.py:29
  18.1 1.1 %collective-permute-done.1 = f32[9,7,4,4,1]{0,3,4,2,1:T(4,128)S(1)} collective-permute-done((f32[9,7,4,4,1]{0,3,4,2,1:T(4,128)S(1)}, f32[9,7,4,4,1]{0,3,4,2,1:T(4,128)S(1)}, u32[]{:S(2)}, u32[]{:S(2)}) %collective-permute-start.1) | collective-permute-done | bytes 4064 | tf_op jit(solution)/shard_map/ppermute | solution.py:26
  19.1 0.8 %copy.20 = f32[9,7,4,4,1]{4,0,3,2,1:T(8,128)S(1)} copy(f32[9,7,4,4,1]{0,3,4,2,1:T(4,128)S(1)} %collective-permute-done.1) | data formatting | bytes 8064 | tf_op jit(solution)/shard_map/ppermute | solution.py:26
  19.9 0.8 %fusion.14 = f32[9,7,4,4,128]{4,0,3,2,1:T(8,128)S(1)} fusion(f32[9,7,4,4,1]{4,0,3,2,1:T(8,128)S(1)} %copy.18, f32[9,7,4,4,128]{4,0,3,2,1:T(8,128)S(1)} %bitcast.33, f32[9,7,4,4,1]{4,0,3,2,1:T(8,128)S(1)} %copy.20), kind=kLoop, calls=%fused_computation.24 | loop fusion | flops 387072 | bytes 1040256 | tf_op jit(solution)/shard_map/sub | solution.py:75
  20.7 2.4 %fusion.12 = f32[9,4,4,128,7]{3,4,2,1,0:T(8,128)} fusion(f32[9,7,4,4,128]{4,0,3,2,1:T(8,128)S(1)} %fusion.14, f32[1,7,7]{2,0,1:T(1,128)} %param.7), kind=kOutput, calls=%fused_computation.22 | convolution fusion | flops 10838016 | bytes 1032388 | tf_op jit(solution)/shard_map/fg,tgasc->tfasc/dot_general | solution.py:74
  23.2 0.0 copy-done
  23.2 0.0 collective-permute-done.4
  23.2 20.6 %all_gather.3 = f32[9,7,4,512]{3,0,2,1:T(8,128)S(1)} all-gather(f32[9,7,4,128]{3,0,2,1:T(8,128)} %collective-permute-done.4), channel_id=1, replica_groups=mesh['row'=2,'sec'=4,'span'=4] {'sec'}, dimensions={3}, use_global_device_ids=true | all-gather | bytes 645120 | tf_op jit(solution)/shard_map/all_gather | solution.py:56
  43.8 7.5 %copy.23 = f32[9,7,4,512]{1,2,3,0:T(4,128)} copy(f32[9,7,4,512]{3,0,2,1:T(8,128)S(1)} %all_gather.3) | data formatting | bytes 1032192 | tf_op jit(solution)/shard_map/all_gather | solution.py:56
  51.3 16.5 %gather_fusion = f32[1152,7,4]{1,2,0:T(4,128)} fusion(f32[9,7,4,512]{1,2,3,0:T(4,128)} %copy.23, s32[1152]{0:T(1024)S(1)} %fusion.22), kind=kCustom, calls=%fused_computation | custom fusion | bytes 267264 | tf_op jit(solution)/shard_map/vmap(jit(_take))/gather | solution.py:59
  67.8 2.9 %copy.28 = f32[9,128,7,4]{1,0,3,2:T(8,128)S(1)} copy(f32[9,128,7,4]{2,3,1,0:T(4,128)} %bitcast.35) | data formatting | bytes 258048 | tf_op jit(solution)/shard_map/vmap(jit(_take))/gather | solution.py:59
  70.7 0.0 copy-done.1
  70.7 0.0 collective-permute-done.3
  70.7 0.0 collective-permute-done.2
  70.7 3.6 %fusion.9 = f32[1,9,7,4,4,128]{5,1,4,3,2,0:T(8,128)S(1)} fusion(f32[9,7,4,4,128]{4,0,3,2,1:T(8,128)S(1)} %bitcast.34, f32[9,7,4,1,128]{4,0,3,2,1:T(8,128)} %collective-permute-done.3, f32[9,7,4,1,128]{4,0,3,2,1:T(8,128)} %collective-permute-done.2, f32[9,7,1,4,128]{4,0,3,2,1:T(8,128)S(1)} %bitcast_select_fusion, f32[9,7,3,4,128]{4,0,3,2,1:T(8,128)} %get-tuple-element.6, ...), kind=kOutput, calls=%fused_computation.12 | convolution fusion | flops 16774902 | bytes 2725764 | tf_op jit(solution)/shard_map/tu,ufasc->tfasc/dot_general | solution.py:71
  74.3 1.0 %copy.25 = f32[1,9,7,4,4,128]{5,4,3,2,1,0:T(4,128)} copy(f32[1,9,7,4,4,128]{5,1,4,3,2,0:T(8,128)S(1)} %fusion.9) | data formatting | bytes 1032192 | tf_op jit(solution)/shard_map/broadcast_in_dim | solution.py:84
  (6 shorter events, 0.0 us)
Async XLA Ops:
  2.1 68.7 %collective-permute-start.3 = (f32[9,7,4,1,128]{4,0,3,2,1:T(8,128)}, f32[9,7,4,1,128]{4,0,3,2,1:T(8,128)}, u32[]{:S(2)}, u32[]{:S(2)}) collective-permute-start(f32[9,7,4,1,128]{4,0,3,2,1:T(8,128)} %get-tuple-element.10), channel_id=1, source_target_pairs={{0,1},{1,2},{2,3},{4,5},{5,6},{6,7},{8,9},{9,10},{10,11},{12,13},{... | collective-permute-start | bytes 387080 | tf_op jit(solution)/shard_map/ppermute | solution.py:26
  7.7 63.0 %collective-permute-start.2 = (f32[9,7,4,1,128]{4,0,3,2,1:T(8,128)}, f32[9,7,4,1,128]{4,0,3,2,1:T(8,128)}, u32[]{:S(2)}, u32[]{:S(2)}) collective-permute-start(f32[9,7,4,1,128]{4,0,3,2,1:T(8,128)} %get-tuple-element.9), channel_id=1, source_target_pairs={{1,0},{2,1},{3,2},{5,4},{6,5},{7,6},{9,8},{10,9},{11,10},{13,12},{... | collective-permute-start | bytes 387080 | tf_op jit(solution)/shard_map/ppermute | solution.py:29
  9.7 13.5 %collective-permute-start.4 = (f32[9,7,4,128]{3,0,2,1:T(8,128)}, f32[9,7,4,128]{3,0,2,1:T(8,128)}, u32[]{:S(2)}, u32[]{:S(2)}) collective-permute-start(f32[9,7,4,128]{3,0,2,1:T(8,128)} %slice_bitcast_fusion), channel_id=1, source_target_pairs={{0,16},{16,0},{1,17},{17,1},{2,18},{18,2},{3,19},{19,3},{4,20},{20... | collective-permute-start | bytes 387080 | tf_op jit(solution)/shard_map/ppermute | solution.py:16
  10.8 6.5 %collective-permute-start = (f32[9,7,4,4,1]{0,3,4,2,1:T(4,128)S(1)}, f32[9,7,4,4,1]{0,3,4,2,1:T(4,128)S(1)}, u32[]{:S(2)}, u32[]{:S(2)}) collective-permute-start(f32[9,7,4,4,1]{0,3,4,2,1:T(4,128)S(1)} %copy.17), channel_id=1, source_target_pairs={{4,0},{8,4},{12,8},{0,12},{5,1},{9,5},{13,9},{1,13},{6,2},{10,6},{... | collective-permute-start | bytes 12104 | tf_op jit(solution)/shard_map/ppermute | solution.py:29
  14.0 5.1 %collective-permute-start.1 = (f32[9,7,4,4,1]{0,3,4,2,1:T(4,128)S(1)}, f32[9,7,4,4,1]{0,3,4,2,1:T(4,128)S(1)}, u32[]{:S(2)}, u32[]{:S(2)}) collective-permute-start(f32[9,7,4,4,1]{0,3,4,2,1:T(4,128)S(1)} %copy.19), channel_id=1, source_target_pairs={{0,4},{4,8},{8,12},{12,0},{1,5},{5,9},{9,13},{13,1},{2,6},{6,10},{... | collective-permute-start | bytes 12104 | tf_op jit(solution)/shard_map/ppermute | solution.py:26
  19.9 3.2 %copy-start = (f32[9,7,4,4,1]{4,0,3,2,1:T(8,128)}, f32[9,7,4,4,1]{4,0,3,2,1:T(8,128)S(1)}, u32[]{:S(2)}) copy-start(f32[9,7,4,4,1]{4,0,3,2,1:T(8,128)S(1)} %copy.20) | copy-start | bytes 12100
  43.8 26.9 %copy-start.1 = (pred[9,128]{1,0:T(8,128)(4,1)S(1)}, pred[9,128]{1,0:T(8,128)(4,1)}, u32[]{:S(2)}) copy-start(pred[9,128]{1,0:T(8,128)(4,1)} %compare_and_fusion) | copy-start | bytes 3460
  43.8 26.9 %copy-start.2 = (f32[1,4,4,128]{3,2,1,0:T(4,128)S(1)}, f32[1,4,4,128]{3,2,1,0:T(4,128)}, u32[]{:S(2)}) copy-start(f32[1,4,4,128]{3,2,1,0:T(4,128)} %param.6) | copy-start | bytes 24580
where the time goes:
time: 75.7 us; the launch traced here: 75.3 us
  local copies, waits for them, and re-layouts  35.2 us (46%)
  blocking collectives  20.6 us (27%)
  starting transfers between devices  9.43 us (12%)
  matrix products  6.03 us (8%)
  other arithmetic  2.21 us (3%)
  waiting for transfers between devices  1.09 us (1%)
  between operations  0.76 us (1%)
    all_gather x1, blocking collectives, on_device(): whole = lax.all_gather(other, 'sec', axis=3, tiled=True)  20.6 us
    gather x2, local copies, waits for them, and re-layouts, on_device(): jnp.take(block, where, axis=2)  19.4 us
    all_gather x1, local copies, waits for them, and re-layouts, on_device(): whole = lax.all_gather(other, 'sec', axis=3, tiled=True)  7.49 us
    ppermute x2, starting transfers between devices, extended(): lax.ppermute(lax.slice_in_dim(block, block.shape[dim] - width, None, axis...  5.66 us
    ppermute x2, starting transfers between devices, extended(): lax.ppermute(lax.slice_in_dim(block, 0, width, axis=dim), axis, backward)  3.76 us
    dot_general x1, matrix products, on_device(): jnp.einsum('tu,ufasc->tfasc', deriv, flow_field_values, precision=lax.Pre...  3.59 us
    dot_general x1, matrix products, on_device(): jnp.einsum('fg,tgasc->tfasc', jac_row, plus_theta - minus_theta, precisio...  2.44 us
    slice x2, local copies, waits for them, and re-layouts, extended(): lax.slice_in_dim(block, 0, width, axis=dim)  1.59 us
  transfers between devices with their start and end apart: 5, of which 1 were waited for; matrix products, arithmetic and copies ran while one was open for 49% of the time, Pallas kernels for 0%

commit v1 on v0

v1 whole, which is shorter than its diff:
```python
import math

import jax
import jax.numpy as jnp
from jax import lax
from jax.experimental import pallas as pl
from jax.experimental.pallas import tpu as pltpu
from jax.sharding import PartitionSpec as P

VMEM = pl.BlockSpec(memory_space=pltpu.VMEM)
SMEM = pl.BlockSpec(memory_space=pltpu.SMEM)


def pairs(count, first, periodic):
    route = []
    for low in range(first, count, 2):
        high = low + 1
        if high < count or periodic:
            high %= count
            route += [(low, high), (high, low)]
    return route


def crossed(count, distance):
    return [
        (row * count + here, (1 - row) * count + (here ^ distance))
        for row in range(2)
        for here in range(count)
    ]


def pack_kernel(tiles, state_ref, strip_ref, even_ref, odd_ref, edge_ref):
    parity = lax.axis_index("span") % 2
    lane = lax.broadcasted_iota(jnp.int32, (16, 128), 1)
    low = state_ref[pl.ds(0, 4 * tiles, stride=4), :]
    high = state_ref[pl.ds(3, 4 * tiles, stride=4), :]
    even_ref[...] = jnp.where(parity == 0, high, low)
    odd_ref[...] = jnp.where(parity == 0, low, high)

    def step(i, edge):
        block = state_ref[pl.ds(pl.multiple_of(i * 16, 16), 16), :]
        strip_ref[i] = block[12:]
        turned = pltpu.roll(block, 2 * i + 1, 1)
        return jnp.where(lane // 2 == i, turned, edge)

    edge_ref[...] = lax.fori_loop(0, tiles, step, jnp.zeros((16, 128), jnp.float32), unroll=7)


def update_kernel(
    times,
    fields,
    slots,
    state_ref,
    coeff_ref,
    jac_ref,
    omega_ref,
    offset_ref,
    even_ref,
    odd_ref,
    edge_a_ref,
    edge_b_ref,
    *rest,
):
    source_refs, out_ref = rest[:-1], rest[-1]
    sectors = lax.axis_size("sec")
    row = lax.axis_index("row")
    sec = lax.axis_index("sec")
    span_parity = lax.axis_index("span") % 2
    sec_parity = sec % 2
    lane = lax.broadcasted_iota(jnp.int32, (8, 128), 1)
    sub = lax.broadcasted_iota(jnp.int32, (8, 128), 0)
    lower = sub < 4
    bottom = sub % 4 == 0
    top = sub % 4 == 3
    lane4 = lax.broadcasted_iota(jnp.int32, (4, 128), 1)

    edge_a, edge_b = edge_a_ref[...], edge_b_ref[...]
    plus_edge = jnp.where(sec_parity == 0, edge_a, edge_b)
    minus_edge = jnp.where(sec_parity == 0, edge_b, edge_a)
    wide_lane = lax.broadcasted_iota(jnp.int32, (16, 128), 1)
    halo = jnp.where(
        wide_lane % 2 == 0, pltpu.roll(plus_edge, 127, 1), pltpu.roll(minus_edge, 1, 1)
    )
    coeff = [0.1 * coeff_ref[0:8, :], 0.1 * coeff_ref[8:16, :]]
    own = [0.8 - 4.0 * c for c in coeff]
    rate = -0.1 * omega_ref[0]
    weight = [0.0]
    weight += [0.5 * (-1.0) ** m / math.sin(math.pi * m / times) for m in range(1, times)]

    def pick(slot, index):
        if len(source_refs) == 1:
            return source_refs[0][slot, index]
        value = source_refs[0][index]
        for other in range(1, slots):
            value = jnp.where(slot == other, source_refs[other][index], value)
        return value

    def step(t, _):
        offset = offset_ref[t]
        total = sectors * 128
        shift = jnp.where(row == 0, offset, lax.rem(total - offset, total))
        whole, part = shift // 128, shift % 128
        near = lax.rem(sec - whole + sectors, sectors)
        far = lax.rem(sec - whole - 1 + sectors + sectors, sectors)
        if len(source_refs) > 1:
            near, far = near ^ sec, far ^ sec

        def load(u, f, h):
            start = pl.multiple_of((u * fields + f) * 16 + 8 * h, 8)
            return state_ref[pl.ds(start, 8), :]

        centre = [[load(t, f, h) for h in range(2)] for f in range(fields)]
        difference, result = [], []
        for f in range(fields):
            index = t * fields + f
            turned = pltpu.roll(halo, 127 - 2 * index, 1)
            ghost = pick(near, index)
            ghost_far = pick(far, index)
            ghost = pltpu.roll(jnp.where(lane4 >= 128 - part, ghost_far, ghost), part, 1)
            ghost = jnp.concatenate([ghost, ghost], axis=0)
            v0, v1 = centre[f]
            r0, r1 = pltpu.roll(v0, 4, 0), pltpu.roll(v1, 4, 0)
            middle = jnp.where(lower, r0, r1)
            axial = [
                middle + jnp.where(lower, 0.0, r0),
                jnp.where(lower, r1, ghost) + middle,
            ]
            differences, results = [], []
            for h in range(2):
                v = centre[f][h]
                edge = turned[8 * h : 8 * h + 8]
                plus = jnp.where(lane == 127, edge, pltpu.roll(v, 127, 1))
                minus = jnp.where(lane == 0, edge, pltpu.roll(v, 1, 1))
                start = 4 * index + 2 * h
                even = jnp.where(
                    lower, even_ref[pl.ds(start, 1), :], even_ref[pl.ds(start + 1, 1), :]
                )
                odd = jnp.where(
                    lower, odd_ref[pl.ds(start, 1), :], odd_ref[pl.ds(start + 1, 1), :]
                )
                up_halo = jnp.where(span_parity == 0, even, odd)
                down_halo = jnp.where(span_parity == 0, odd, even)
                up = jnp.where(top, up_halo, pltpu.roll(v, 7, 0))
                down = jnp.where(bottom, down_halo, pltpu.roll(v, 1, 0))
                differences.append(plus - minus)
                value = own[h] * v + coeff[h] * ((plus + minus) + (up + down)) + 0.1 * axial[h]
                spectral = jnp.zeros_like(v)
                for m in range(1, times // 2 + 1):
                    before = load(lax.rem(t + times - m, times), f, h)
                    after = load(lax.rem(t + m, times), f, h)
                    spectral = spectral + weight[m] * (before - after)
                results.append(value + rate * spectral)
            difference.append(differences)
            result.append(results)
        for f in range(fields):
            for h in range(2):
                value = result[f][h]
                for g in range(fields):
                    value = value + (-0.05 * jac_ref[f, g]) * difference[g][h]
                start = pl.multiple_of((t * fields + f) * 16 + 8 * h, 8)
                out_ref[pl.ds(start, 8), :] = value
        return 0

    lax.fori_loop(0, times, step, 0)


def on_device(state, viscosity, jacobian, frequency, offsets):
    _, times, fields, axial, spans, cells = state.shape
    tiles = times * fields
    sectors, slabs = lax.axis_size("sec"), lax.axis_size("span")
    flat = state.reshape(tiles * 16, cells)
    strip, even, odd, edge = pl.pallas_call(
        lambda *refs: pack_kernel(tiles, *refs),
        out_shape=[
            jax.ShapeDtypeStruct((tiles, 4, cells), jnp.float32),
            jax.ShapeDtypeStruct((tiles * 4, cells), jnp.float32),
            jax.ShapeDtypeStruct((tiles * 4, cells), jnp.float32),
            jax.ShapeDtypeStruct((16, cells), jnp.float32),
        ],
        in_specs=[VMEM],
        out_specs=[VMEM] * 4,
        name="pack",
    )(flat)
    odd = lax.ppermute(odd, "span", pairs(slabs, 1, False))
    even = lax.ppermute(even, "span", pairs(slabs, 0, False))
    edge_b = lax.ppermute(edge, "sec", pairs(sectors, 1, True))
    edge_a = lax.ppermute(edge, "sec", pairs(sectors, 0, True))
    swapped = lax.ppermute(strip, "row", [(0, 1), (1, 0)])
    if sectors == 4:
        sources = [swapped] + [
            lax.ppermute(strip, ("row", "sec"), crossed(sectors, distance)) for distance in (1, 2, 3)
        ]
    else:
        sources = [lax.all_gather(swapped, "sec")]
    out = pl.pallas_call(
        lambda *refs: update_kernel(times, fields, sectors, *refs),
        out_shape=jax.ShapeDtypeStruct(flat.shape, jnp.float32),
        in_specs=[VMEM, VMEM, SMEM, SMEM, SMEM] + [VMEM] * (4 + len(sources)),
        out_specs=VMEM,
        compiler_params=pltpu.CompilerParams(vmem_limit_bytes=32 * 1024 * 1024),
        name="update",
    )(
        flat,
        viscosity.reshape(16, cells),
        jacobian[0],
        frequency,
        offsets,
        even,
        odd,
        edge_a,
        edge_b,
        *sources,
    )
    return out.reshape(state.shape)


def solution(mesh):
    return jax.shard_map(
        on_device,
        mesh=mesh,
        in_specs=(
            P("row", None, None, None, "span", "sec"),
            P("row", None, "span", "sec"),
            P("row", None, None),
            P("row"),
            P(),
        ),
        out_specs=P("row", None, None, None, "span", "sec"),
        check_vma=False,
    )
```

time: 75.7 us -> 22.7 us (0.30)
  the two profiles are of different devices: /device:TPU:0 before, /device:TPU:16 now
where the time goes in v1:
time: 22.7 us; the launch traced here: 22.6 us
  starting transfers between devices  9.15 us (40%)
  waiting for transfers between devices  6.68 us (29%)
  Pallas kernels  5.38 us (24%)
  between operations  0.71 us (3%)
  local copies, waits for them, and re-layouts  0.66 us (3%)
    ppermute x3, starting transfers between devices, on_device(): lax.ppermute(strip, ('row', 'sec'), crossed(sectors, distance))  3.66 us
    ppermute x1, waiting for transfers between devices, on_device(): odd = lax.ppermute(odd, 'span', pairs(slabs, 1, False))  3.18 us
    pallas_call x1, Pallas kernels, on_device(): pl.pallas_call(lambda *refs: update_kernel(times, fields, sectors, *refs)...  2.83 us
    pallas_call x1, Pallas kernels, on_device(): pl.pallas_call(lambda *refs: pack_kernel(tiles, *refs), out_shape=[jax.Sh...  2.56 us
    ppermute x1, starting transfers between devices, on_device(): odd = lax.ppermute(odd, 'span', pairs(slabs, 1, False))  1.91 us
    ppermute x1, waiting for transfers between devices, on_device(): even = lax.ppermute(even, 'span', pairs(slabs, 0, False))  1.86 us
    ppermute x1, starting transfers between devices, on_device(): even = lax.ppermute(even, 'span', pairs(slabs, 0, False))  1.6 us
    ppermute x1, waiting for transfers between devices, on_device(): edge_b = lax.ppermute(edge, 'sec', pairs(sectors, 1, True))  1.59 us
  transfers between devices with their start and end apart: 8, of which 3 were waited for; matrix products, arithmetic and copies ran while one was open for 0% of the time, Pallas kernels for 0%

profile of v1, /device:TPU:16, one launch (start us, length us, event | category | flops | bytes accessed | tf_op | source)
XLA Modules:
  0.0 22.6 jit_solution(11800530788633922658)
XLA Ops:
  0.0 0.0 copy-start
  0.0 2.6 %pack.1 = (f32[63,4,128]{2,1,0:T(4,128)}, f32[252,128]{1,0:T(8,128)}, f32[252,128]{1,0:T(8,128)}, f32[16,128]{1,0:T(8,128)}) custom-call(f32[1008,128]{1,0:T(8,128)} %bitcast.6), custom_call_target="tpu_custom_call" | custom-call | tf_op jit(solution)/shard_map/pack/pallas_call | solution.py:172
  2.6 0.0 copy-start.3
  2.6 1.9 %collective-permute-start.7 = (f32[63,4,128]{2,1,0:T(4,128)}, f32[63,4,128]{2,1,0:T(4,128)S(1)}, u32[]{:S(2)}, u32[]{:S(2)}) collective-permute-start(f32[63,4,128]{2,1,0:T(4,128)} %get-tuple-element.12), channel_id=1, source_target_pairs={{0,28},{4,24},{8,20},{12,16},{16,12},{20,8},{24,4},{28,0},{1,29},{... | collective-permute-start | bytes 387080 | tf_op jit(solution)/shard_map/ppermute | solution.py:191
  4.4 0.6 %collective-permute-start.3 = (f32[16,128]{1,0:T(8,128)}, f32[16,128]{1,0:T(8,128)S(1)}, u32[]{:S(2)}, u32[]{:S(2)}) collective-permute-start(f32[16,128]{1,0:T(8,128)} %get-tuple-element.11), channel_id=1, source_target_pairs={{4,8},{8,4},{12,0},{0,12},{5,9},{9,5},{13,1},{1,13},{6,10},{10,6},... | collective-permute-start | bytes 24584 | tf_op jit(solution)/shard_map/ppermute | solution.py:186
  5.1 1.3 %collective-permute-start.2 = (f32[16,128]{1,0:T(8,128)}, f32[16,128]{1,0:T(8,128)S(1)}, u32[]{:S(2)}, u32[]{:S(2)}) collective-permute-start(f32[16,128]{1,0:T(8,128)} %get-tuple-element.11), channel_id=1, source_target_pairs={{0,4},{4,0},{8,12},{12,8},{1,5},{5,1},{9,13},{13,9},{2,6},{6,2},{1... | collective-permute-start | bytes 24584 | tf_op jit(solution)/shard_map/ppermute | solution.py:187
  6.4 1.3 %collective-permute-start.6 = (f32[63,4,128]{2,1,0:T(4,128)}, f32[63,4,128]{2,1,0:T(4,128)S(1)}, u32[]{:S(2)}, u32[]{:S(2)}) collective-permute-start(f32[63,4,128]{2,1,0:T(4,128)} %get-tuple-element.12), channel_id=1, source_target_pairs={{0,24},{4,28},{8,16},{12,20},{16,8},{20,12},{24,0},{28,4},{1,25},{... | collective-permute-start | bytes 387080 | tf_op jit(solution)/shard_map/ppermute | solution.py:191
  7.7 0.5 %collective-permute-start.5 = (f32[63,4,128]{2,1,0:T(4,128)}, f32[63,4,128]{2,1,0:T(4,128)S(1)}, u32[]{:S(2)}, u32[]{:S(2)}) collective-permute-start(f32[63,4,128]{2,1,0:T(4,128)} %get-tuple-element.12), channel_id=1, source_target_pairs={{0,20},{4,16},{8,28},{12,24},{16,4},{20,0},{24,12},{28,8},{1,21},{... | collective-permute-start | bytes 387080 | tf_op jit(solution)/shard_map/ppermute | solution.py:191
  8.2 1.6 %collective-permute-done.3.refs_8_ = f32[16,128]{1,0:T(8,128)S(1)} collective-permute-done((f32[16,128]{1,0:T(8,128)}, f32[16,128]{1,0:T(8,128)S(1)}, u32[]{:S(2)}, u32[]{:S(2)}) %collective-permute-start.3) | collective-permute-done | bytes 8224 | tf_op jit(solution)/shard_map/ppermute | solution.py:186
  9.8 0.0 collective-permute-start.4
  9.8 0.0 collective-permute-done.2.refs_7_
  9.8 0.0 copy-start.1
  9.8 1.6 %collective-permute-start = (f32[252,128]{1,0:T(8,128)}, f32[252,128]{1,0:T(8,128)S(1)}, u32[]{:S(2)}, u32[]{:S(2)}) collective-permute-start(f32[252,128]{1,0:T(8,128)} %get-tuple-element.9), channel_id=1, source_target_pairs={{0,1},{1,0},{2,3},{3,2},{4,5},{5,4},{6,7},{7,6},{8,9},{9,8},{10,11... | collective-permute-start | bytes 387080 | tf_op jit(solution)/shard_map/ppermute | solution.py:185
  11.4 0.0 collective-permute-done.7.refs_12_
  11.4 1.9 %collective-permute-start.1 = (f32[252,128]{1,0:T(8,128)}, f32[252,128]{1,0:T(8,128)S(1)}, u32[]{:S(2)}, u32[]{:S(2)}) collective-permute-start(f32[252,128]{1,0:T(8,128)} %get-tuple-element.10), channel_id=1, source_target_pairs={{1,2},{2,1},{5,6},{6,5},{9,10},{10,9},{13,14},{14,13},{17,18},{18,... | collective-permute-start | bytes 387080 | tf_op jit(solution)/shard_map/ppermute | solution.py:184
  14.0 0.0 copy-done.3
  14.0 0.0 collective-permute-done.6.refs_11_
  14.0 0.0 collective-permute-done.5.refs_10_
  14.1 0.0 collective-permute-done.4.refs_9_
  14.1 1.9 %collective-permute-done.refs_5_ = f32[252,128]{1,0:T(8,128)S(1)} collective-permute-done((f32[252,128]{1,0:T(8,128)}, f32[252,128]{1,0:T(8,128)S(1)}, u32[]{:S(2)}, u32[]{:S(2)}) %collective-permute-start) | collective-permute-done | bytes 129056 | tf_op jit(solution)/shard_map/ppermute | solution.py:185
  15.9 3.2 %collective-permute-done.1.refs_6_ = f32[252,128]{1,0:T(8,128)S(1)} collective-permute-done((f32[252,128]{1,0:T(8,128)}, f32[252,128]{1,0:T(8,128)S(1)}, u32[]{:S(2)}, u32[]{:S(2)}) %collective-permute-start.1) | collective-permute-done | bytes 129056 | tf_op jit(solution)/shard_map/ppermute | solution.py:184
  19.1 0.0 copy-start.2
  19.1 0.0 copy-done
  19.1 0.0 copy-done.1
  19.1 0.6 %copy-done.2 = s32[9]{0:T(128)S(1)} copy-done((s32[9]{0:T(128)S(1)}, s32[9]{0:T(128)}, u32[]{:S(2)}) %copy-start.2) | copy-done | bytes 60
  19.8 2.8 %update.1 = f32[1008,128]{1,0:T(8,128)} custom-call(f32[1008,128]{1,0:T(8,128)S(1)} %bitcast.7, f32[16,128]{1,0:T(8,128)S(1)} %bitcast.9, f32[7,7]{1,0:T(8,128)S(1)} %bitcast.8, f32[1]{0:T(128)S(6)} %copy.9.refs_3_, s32[9]{0:T(128)S(1)} %copy-done.2, f32[252,128]{1,0:T(8,128)S(1)} %collective-permute-done.refs_5_, ...), custom_call_target="tpu_custom_call" | custom-call | tf_op jit(solution)/shard_map/update/pallas_call | solution.py:195
  (1 shorter events, 0.0 us)
Async XLA Ops:
  0.0 19.1 %copy-start = (f32[1,9,7,4,4,128]{5,4,3,2,1,0:T(4,128)S(1)}, f32[1,9,7,4,4,128]{5,4,3,2,1,0:T(4,128)}, u32[]{:S(2)}) copy-start(f32[1,9,7,4,4,128]{5,4,3,2,1,0:T(4,128)} %param.5) | copy-start | bytes 1548292
  2.6 11.5 %copy-start.3 = (f32[1,7,7]{2,0,1:T(1,128)S(1)}, f32[1,7,7]{2,0,1:T(1,128)}, u32[]{:S(2)}) copy-start(f32[1,7,7]{2,0,1:T(1,128)} %param.7) | copy-start | bytes 592
  2.6 8.9 %collective-permute-start.7 = (f32[63,4,128]{2,1,0:T(4,128)}, f32[63,4,128]{2,1,0:T(4,128)S(1)}, u32[]{:S(2)}, u32[]{:S(2)}) collective-permute-start(f32[63,4,128]{2,1,0:T(4,128)} %get-tuple-element.12), channel_id=1, source_target_pairs={{0,28},{4,24},{8,20},{12,16},{16,12},{20,8},{24,4},{28,0},{1,29},{... | collective-permute-start | bytes 387080 | tf_op jit(solution)/shard_map/ppermute | solution.py:191
  4.4 5.3 %collective-permute-start.3 = (f32[16,128]{1,0:T(8,128)}, f32[16,128]{1,0:T(8,128)S(1)}, u32[]{:S(2)}, u32[]{:S(2)}) collective-permute-start(f32[16,128]{1,0:T(8,128)} %get-tuple-element.11), channel_id=1, source_target_pairs={{4,8},{8,4},{12,0},{0,12},{5,9},{9,5},{13,1},{1,13},{6,10},{10,6},... | collective-permute-start | bytes 24584 | tf_op jit(solution)/shard_map/ppermute | solution.py:186
  5.1 4.8 %collective-permute-start.2 = (f32[16,128]{1,0:T(8,128)}, f32[16,128]{1,0:T(8,128)S(1)}, u32[]{:S(2)}, u32[]{:S(2)}) collective-permute-start(f32[16,128]{1,0:T(8,128)} %get-tuple-element.11), channel_id=1, source_target_pairs={{0,4},{4,0},{8,12},{12,8},{1,5},{5,1},{9,13},{13,9},{2,6},{6,2},{1... | collective-permute-start | bytes 24584 | tf_op jit(solution)/shard_map/ppermute | solution.py:187
  6.4 7.6 %collective-permute-start.6 = (f32[63,4,128]{2,1,0:T(4,128)}, f32[63,4,128]{2,1,0:T(4,128)S(1)}, u32[]{:S(2)}, u32[]{:S(2)}) collective-permute-start(f32[63,4,128]{2,1,0:T(4,128)} %get-tuple-element.12), channel_id=1, source_target_pairs={{0,24},{4,28},{8,16},{12,20},{16,8},{20,12},{24,0},{28,4},{1,25},{... | collective-permute-start | bytes 387080 | tf_op jit(solution)/shard_map/ppermute | solution.py:191
  7.7 6.3 %collective-permute-start.5 = (f32[63,4,128]{2,1,0:T(4,128)}, f32[63,4,128]{2,1,0:T(4,128)S(1)}, u32[]{:S(2)}, u32[]{:S(2)}) collective-permute-start(f32[63,4,128]{2,1,0:T(4,128)} %get-tuple-element.12), channel_id=1, source_target_pairs={{0,20},{4,16},{8,28},{12,24},{16,4},{20,0},{24,12},{28,8},{1,21},{... | collective-permute-start | bytes 387080 | tf_op jit(solution)/shard_map/ppermute | solution.py:191
  9.8 4.3 %collective-permute-start.4 = (f32[63,4,128]{2,1,0:T(4,128)}, f32[63,4,128]{2,1,0:T(4,128)S(1)}, u32[]{:S(2)}, u32[]{:S(2)}) collective-permute-start(f32[63,4,128]{2,1,0:T(4,128)} %get-tuple-element.12), channel_id=1, source_target_pairs={{0,16},{16,0},{1,17},{17,1},{2,18},{18,2},{3,19},{19,3},{4,20},{20... | collective-permute-start | bytes 387080 | tf_op jit(solution)/shard_map/ppermute | solution.py:188
  9.8 9.3 %copy-start.1 = (f32[1,4,4,128]{3,2,1,0:T(4,128)S(1)}, f32[1,4,4,128]{3,2,1,0:T(4,128)}, u32[]{:S(2)}) copy-start(f32[1,4,4,128]{3,2,1,0:T(4,128)} %param.6) | copy-start | bytes 24580
  9.8 6.1 %collective-permute-start = (f32[252,128]{1,0:T(8,128)}, f32[252,128]{1,0:T(8,128)S(1)}, u32[]{:S(2)}, u32[]{:S(2)}) collective-permute-start(f32[252,128]{1,0:T(8,128)} %get-tuple-element.9), channel_id=1, source_target_pairs={{0,1},{1,0},{2,3},{3,2},{4,5},{5,4},{6,7},{7,6},{8,9},{9,8},{10,11... | collective-permute-start | bytes 387080 | tf_op jit(solution)/shard_map/ppermute | solution.py:185
  11.4 7.7 %collective-permute-start.1 = (f32[252,128]{1,0:T(8,128)}, f32[252,128]{1,0:T(8,128)S(1)}, u32[]{:S(2)}, u32[]{:S(2)}) collective-permute-start(f32[252,128]{1,0:T(8,128)} %get-tuple-element.10), channel_id=1, source_target_pairs={{1,2},{2,1},{5,6},{6,5},{9,10},{10,9},{13,14},{14,13},{17,18},{18,... | collective-permute-start | bytes 387080 | tf_op jit(solution)/shard_map/ppermute | solution.py:184
  19.1 0.7 %copy-start.2 = (s32[9]{0:T(128)S(1)}, s32[9]{0:T(128)}, u32[]{:S(2)}) copy-start(s32[9]{0:T(128)} %refs_4_.1) | copy-start | bytes 112

commit v2 on v1

v2 whole, which is shorter than its diff:
```python
import math

import jax
import jax.numpy as jnp
from jax import lax
from jax.experimental import pallas as pl
from jax.experimental.pallas import tpu as pltpu
from jax.sharding import PartitionSpec as P

VMEM = pl.BlockSpec(memory_space=pltpu.VMEM)
SMEM = pl.BlockSpec(memory_space=pltpu.SMEM)
ANY = pl.BlockSpec(memory_space=pl.ANY)
LIMIT = pltpu.CompilerParams(vmem_limit_bytes=32 * 1024 * 1024)


def sector_pairs(count, first):
    return [
        pair
        for low in range(first, count, 2)
        for pair in ((low, (low + 1) % count), ((low + 1) % count, low))
    ]


def slab_pairs(count, first):
    route = []
    for row in range(2):
        for here in range(count):
            there = here ^ 1 if first == 0 else ((here - 1) ^ 1) + 1
            if 0 <= there < count:
                route.append((row * count + here, row * count + there))
            else:
                route.append((row * count + here, (1 - row) * count + here))
    return route


def collect_kernel(tiles, source_ref, state_ref, strip_ref, even_ref, odd_ref, sem):
    copy = pltpu.make_async_copy(source_ref, state_ref, sem)
    copy.start()
    slab, slabs = lax.axis_index("span"), lax.axis_size("span")
    parity = lax.rem(slab, 2)
    paired_even = (slab ^ 1) < slabs
    paired_odd = jnp.logical_and(slab > 0, ((slab - 1) ^ 1) + 1 < slabs)
    copy.wait()
    low = state_ref[pl.ds(0, 4 * tiles, stride=4), :]
    high = state_ref[pl.ds(3, 4 * tiles, stride=4), :]
    even_ref[...] = jnp.where(paired_even, jnp.where(parity == 0, high, low), 0.0)
    odd_ref[...] = jnp.where(paired_odd, jnp.where(parity == 0, low, high), 0.0)

    def step(i, _):
        strip_ref[i] = state_ref[pl.ds(i * 16 + 12, 4), :]
        return 0

    lax.fori_loop(0, tiles, step, 0, unroll=9)


def edge_kernel(tiles, state_ref, edge_ref):
    lane = lax.broadcasted_iota(jnp.int32, (16, 128), 1)

    def step(i, edge):
        block = state_ref[pl.ds(pl.multiple_of(i * 16, 16), 16), :]
        return jnp.where(lane // 2 == i, pltpu.roll(block, 2 * i + 1, 1), edge)

    edge = lax.fori_loop(0, tiles, step, jnp.zeros((16, 128), jnp.float32), unroll=7)
    for a in range(4):
        edge_ref[a] = edge[4 * a : 4 * a + 4]


def inner_kernel(
    times,
    fields,
    state_ref,
    coeff_ref,
    jac_ref,
    omega_ref,
    offset_ref,
    _,
    partial_ref,
    mix_ref,
    place_ref,
):
    sectors = lax.axis_size("sec")
    row, sec = lax.axis_index("row"), lax.axis_index("sec")
    lane = lax.broadcasted_iota(jnp.int32, (8, 128), 1)
    sub = lax.broadcasted_iota(jnp.int32, (8, 128), 0)
    lower = sub < 4
    bottom = sub % 4 == 0
    top = sub % 4 == 3
    coeff = [0.1 * coeff_ref[0:8, :], 0.1 * coeff_ref[8:16, :]]
    own = [0.8 - 4.0 * c for c in coeff]
    rate = -0.1 * omega_ref[0]
    weight = [0.0]
    weight += [0.5 * (-1.0) ** m / math.sin(math.pi * m / times) for m in range(1, times)]

    field = (lane // 2) % fields
    sign = jnp.where(lane % 2 == 0, -0.05, 0.05)
    for distance in range(1 - fields, fields):
        mix = jnp.zeros((8, 128), jnp.float32)
        for f in range(max(0, distance), min(fields, fields + distance)):
            mix = jnp.where(field == f, jac_ref[f, f - distance], mix)
        mix_ref[fields - 1 + distance] = sign * mix

    def step(t, _):
        offset = offset_ref[t]
        total = sectors * 128
        shift = jnp.where(row == 0, offset, lax.rem(total - offset, total))
        whole = shift // 128
        near = lax.rem(sec - whole + sectors, sectors)
        far = lax.rem(sec - whole - 1 + 2 * sectors, sectors)
        if sectors == 4:
            near, far = near ^ sec, far ^ sec
        place_ref[3 * t] = near
        place_ref[3 * t + 1] = far
        place_ref[3 * t + 2] = shift - 128 * whole

        def load(u, f, h):
            start = pl.multiple_of((u * fields + f) * 16 + 8 * h, 8)
            return state_ref[pl.ds(start, 8), :]

        difference, result = [], []
        for f in range(fields):
            v0, v1 = load(t, f, 0), load(t, f, 1)
            r0, r1 = pltpu.roll(v0, 4, 0), pltpu.roll(v1, 4, 0)
            middle = jnp.where(lower, r0, r1)
            axial = [middle + jnp.where(lower, 0.0, r0), jnp.where(lower, r1, 0.0) + middle]
            differences, results = [], []
            for h, v in enumerate((v0, v1)):
                plus = jnp.where(lane == 127, 0.0, pltpu.roll(v, 127, 1))
                minus = jnp.where(lane == 0, 0.0, pltpu.roll(v, 1, 1))
                up = jnp.where(top, 0.0, pltpu.roll(v, 7, 0))
                down = jnp.where(bottom, 0.0, pltpu.roll(v, 1, 0))
                differences.append(plus - minus)
                value = own[h] * v + coeff[h] * ((plus + minus) + (up + down)) + 0.1 * axial[h]
                spectral = jnp.zeros_like(v)
                for m in range(1, times // 2 + 1):
                    before = load(lax.rem(t + times - m, times), f, h)
                    after = load(lax.rem(t + m, times), f, h)
                    spectral = spectral + weight[m] * (before - after)
                results.append(value + rate * spectral)
            difference.append(differences)
            result.append(results)
        for f in range(fields):
            for h in range(2):
                value = result[f][h]
                for g in range(fields):
                    value = value + (-0.05 * jac_ref[f, g]) * difference[g][h]
                start = pl.multiple_of((t * fields + f) * 16 + 8 * h, 8)
                partial_ref[pl.ds(start, 8), :] = value
        return 0

    lax.fori_loop(0, times, step, 0)


def outer_kernel(
    times,
    fields,
    slots,
    partial_ref,
    mix_ref,
    place_ref,
    coeff_ref,
    even_ref,
    odd_ref,
    edge_a_ref,
    edge_b_ref,
    *rest,
):
    source_refs, (out_ref, span_ref, total_ref, sems) = rest[:-4], rest[-4:]
    tiles = times * fields
    sec_parity = lax.rem(lax.axis_index("sec"), 2)
    span_parity = lax.rem(lax.axis_index("span"), 2)
    lane = lax.broadcasted_iota(jnp.int32, (8, 128), 1)
    sub = lax.broadcasted_iota(jnp.int32, (8, 128), 0)
    lane4 = lax.broadcasted_iota(jnp.int32, (4, 128), 1)
    border = jnp.logical_or(sub % 4 == 0, sub % 4 == 3)
    lower = sub < 4
    outside = jnp.logical_or(lane == 0, lane == 127)
    sides = lane % 2 == 0

    even, odd = even_ref[...], odd_ref[...]
    coeff_low = 0.1 * coeff_ref[pl.ds(0, 4, stride=4), :]
    coeff_high = 0.1 * coeff_ref[pl.ds(3, 4, stride=4), :]
    up = jnp.where(span_parity == 0, even, odd).reshape(tiles, 4, 128) * coeff_high[None]
    down = jnp.where(span_parity == 0, odd, even).reshape(tiles, 4, 128) * coeff_low[None]
    span_ref[pl.ds(3, 4 * tiles, stride=4), :] = up.reshape(4 * tiles, 128)
    span_ref[pl.ds(0, 4 * tiles, stride=4), :] = down.reshape(4 * tiles, 128)

    edges = []
    for h in range(2):
        edge_a = jnp.concatenate([edge_a_ref[tiles_at] for tiles_at in (2 * h, 2 * h + 1)], axis=0)
        edge_b = jnp.concatenate([edge_b_ref[tiles_at] for tiles_at in (2 * h, 2 * h + 1)], axis=0)
        plus_edge = jnp.where(sec_parity == 0, edge_a, edge_b)
        minus_edge = jnp.where(sec_parity == 0, edge_b, edge_a)
        halo = jnp.where(sides, pltpu.roll(plus_edge, 127, 1), pltpu.roll(minus_edge, 1, 1))
        coeff = 0.1 * coeff_ref[8 * h : 8 * h + 8, :]
        term = jnp.where(sides, coeff[:, 127:128], coeff[:, 0:1]) * halo
        for distance in range(1 - fields, fields):
            term = term + mix_ref[fields - 1 + distance] * pltpu.roll(halo, (2 * distance) % 128, 1)
        edges.append(term)

    def pick(slot, index):
        if len(source_refs) == 1:
            return source_refs[0][slot, index]
        value = source_refs[0][index]
        for other in range(1, slots):
            value = jnp.where(slot == other, source_refs[other][index], value)
        return value

    def piece(t):
        rows = pl.ds(pl.multiple_of(t * fields * 16, 16), fields * 16)
        return pltpu.make_async_copy(total_ref.at[rows, :], out_ref.at[rows, :], sems.at[t])

    def step(t, _):
        near, far, part = place_ref[3 * t], place_ref[3 * t + 1], place_ref[3 * t + 2]
        for f in range(fields):
            index = t * fields + f
            ghost = jnp.where(lane4 >= 128 - part, pick(far, index), pick(near, index))
            ghost = pltpu.roll(ghost, part, 1)
            ghost = jnp.concatenate([ghost, ghost], axis=0)
            for h in range(2):
                rows = pl.ds(pl.multiple_of(index * 16 + 8 * h, 8), 8)
                value = partial_ref[rows, :] + jnp.where(border, span_ref[rows, :], 0.0)
                value = value + jnp.where(outside, pltpu.roll(edges[h], 127 - 2 * index, 1), 0.0)
                if h == 1:
                    value = value + jnp.where(lower, 0.0, 0.1 * ghost)
                total_ref[rows, :] = value
        piece(t).start()
        return 0

    lax.fori_loop(0, times, step, 0)
    for t in range(times):
        piece(t).wait()


def on_device(state, viscosity, jacobian, frequency, offsets):
    _, times, fields, axial, spans, cells = state.shape
    tiles = times * fields
    sectors, slabs = lax.axis_size("sec"), lax.axis_size("span")
    flat = state.reshape(tiles * 16, cells)
    coeff = viscosity.reshape(16, cells)
    f32 = jnp.float32
    local, strip, even, odd = pl.pallas_call(
        lambda *refs: collect_kernel(tiles, *refs),
        out_shape=[
            pltpu.VMEM((tiles * 16, cells), f32),
            pltpu.VMEM((tiles, 4, cells), f32),
            pltpu.VMEM((tiles * 4, cells), f32),
            pltpu.VMEM((tiles * 4, cells), f32),
        ],
        in_specs=[ANY],
        out_specs=[VMEM] * 4,
        scratch_shapes=[pltpu.SemaphoreType.DMA],
        compiler_params=LIMIT,
        name="collect",
    )(flat)
    swapped = lax.ppermute(strip, "row", [(0, 1), (1, 0)])
    edge = pl.pallas_call(
        lambda *refs: edge_kernel(tiles, *refs),
        out_shape=pltpu.VMEM((4, 4, cells), f32),
        in_specs=[VMEM],
        out_specs=VMEM,
        compiler_params=LIMIT,
        name="edges",
    )(local)
    packed = jnp.concatenate([swapped, edge], axis=0)
    even = lax.ppermute(even, ("row", "span"), slab_pairs(slabs, 0))
    odd = lax.ppermute(odd, ("row", "span"), slab_pairs(slabs, 1))
    if sectors == 4:
        near = [
            lax.ppermute(packed, "sec", [(k, k ^ distance) for k in range(sectors)])
            for distance in (1, 2, 3)
        ]
        sources = [swapped] + near
        edge_a = edge_b = None
        edge_a, edge_b = near[0][tiles:], near[2][tiles:]
    else:
        sources = [lax.all_gather(swapped, "sec")]
        edge_a = lax.ppermute(edge, "sec", sector_pairs(sectors, 0))
        edge_b = lax.ppermute(edge, "sec", sector_pairs(sectors, 1))
    partial, mix, place = pl.pallas_call(
        lambda *refs: inner_kernel(times, fields, *refs),
        out_shape=[
            pltpu.VMEM((tiles * 16, cells), f32),
            pltpu.VMEM((2 * fields - 1, 8, cells), f32),
            pltpu.SMEM((3 * times,), jnp.int32),
        ],
        in_specs=[VMEM, VMEM, SMEM, SMEM, SMEM, ANY],
        out_specs=[VMEM, VMEM, SMEM],
        compiler_params=LIMIT,
        cost_estimate=pl.CostEstimate(
            flops=tiles * 16 * cells * 50, bytes_accessed=tiles * 16 * cells * 8, transcendentals=0
        ),
        name="inner",
    )(local, coeff, jacobian[0], frequency, offsets, packed)
    out = pl.pallas_call(
        lambda *refs: outer_kernel(times, fields, sectors, *refs),
        out_shape=jax.ShapeDtypeStruct(flat.shape, f32),
        in_specs=[VMEM, VMEM, SMEM] + [VMEM] * (5 + len(sources)),
        out_specs=ANY,
        scratch_shapes=[
            pltpu.VMEM((tiles * 16, cells), f32),
            pltpu.VMEM((tiles * 16, cells), f32),
            pltpu.SemaphoreType.DMA((times,)),
        ],
        compiler_params=LIMIT,
        name="outer",
    )(partial, mix, place, coeff, even, odd, edge_a, edge_b, *sources)
    return out.reshape(state.shape)


def solution(mesh):
    return jax.shard_map(
        on_device,
        mesh=mesh,
        in_specs=(
            P("row", None, None, None, "span", "sec"),
            P("row", None, "span", "sec"),
            P("row", None, None),
            P("row"),
            P(),
        ),
        out_specs=P("row", None, None, None, "span", "sec"),
        check_vma=False,
    )
```

time: 22.7 us -> 16.1 us (0.71)
  the two profiles are of different devices: /device:TPU:16 before, /device:TPU:0 now
where the time goes in v2:
time: 16.1 us; the launch traced here: 15.9 us
  starting transfers between devices  7.01 us (44%)
  Pallas kernels  4.84 us (30%)
  local copies, waits for them, and re-layouts  1.7 us (11%)
  waiting for transfers between devices  1.59 us (10%)
  between operations  0.75 us (5%)
    ppermute x3, starting transfers between devices, on_device(): lax.ppermute(packed, 'sec', [(k, k ^ distance) for k in range(sectors)])  4.51 us
    ppermute x1, starting transfers between devices, on_device(): even = lax.ppermute(even, ('row', 'span'), slab_pairs(slabs, 0))  1.98 us
    pallas_call x1, Pallas kernels, on_device(): pl.pallas_call(lambda *refs: outer_kernel(times, fields, sectors, *refs),...  1.83 us
    pallas_call x1, Pallas kernels, on_device(): pl.pallas_call(lambda *refs: inner_kernel(times, fields, *refs), out_shap...  1.83 us
    unnamed x9, local copies, waits for them, and re-layouts  1.69 us
    ppermute x3, waiting for transfers between devices, on_device(): lax.ppermute(packed, 'sec', [(k, k ^ distance) for k in range(sectors)])  1.36 us
    pallas_call x1, Pallas kernels, on_device(): pl.pallas_call(lambda *refs: edge_kernel(tiles, *refs), out_shape=pltpu.V...  0.75 us
    ppermute x1, starting transfers between devices, on_device(): swapped = lax.ppermute(strip, 'row', [(0, 1), (1, 0)])  0.52 us
  transfers between devices with their start and end apart: 6, of which 2 were waited for; matrix products, arithmetic and copies ran while one was open for 0% of the time, Pallas kernels for 16%

profile of v2, /device:TPU:0, one launch (start us, length us, event | category | flops | bytes accessed | tf_op | source)
XLA Modules:
  0.0 15.9 jit_solution(17056212460086400326)
XLA Ops:
  0.0 0.0 copy-start
  0.0 1.0 %copy-done = f32[1,9,7,4,4,128]{5,4,3,2,1,0:T(4,128)S(1)} copy-done((f32[1,9,7,4,4,128]{5,4,3,2,1,0:T(4,128)S(1)}, f32[1,9,7,4,4,128]{5,4,3,2,1,0:T(4,128)}, u32[]{:S(2)}) %copy-start) | copy-done | bytes 516120
  1.0 0.4 %collect.1 = (f32[1008,128]{1,0:T(8,128)S(1)}, f32[63,4,128]{2,1,0:T(4,128)S(1)}, f32[252,128]{1,0:T(8,128)S(1)}, f32[252,128]{1,0:T(8,128)S(1)}) custom-call(f32[1008,128]{1,0:T(8,128)S(1)} %bitcast.6), custom_call_target="tpu_custom_call" | custom-call | tf_op jit(solution)/shard_map/collect/pallas_call | solution.py:241
  1.5 0.5 %collective-permute-start = (f32[63,4,128]{2,1,0:T(4,128)S(1)}, f32[63,4,128]{2,1,0:T(4,128)S(1)}, u32[]{:S(2)}, u32[]{:S(2)}) collective-permute-start(f32[63,4,128]{2,1,0:T(4,128)S(1)} %get-tuple-element.13), channel_id=1, source_target_pairs={{0,16},{16,0},{1,17},{17,1},{2,18},{18,2},{3,19},{19,3},{4,20},{20... | collective-permute-start | bytes 387080 | tf_op jit(solution)/shard_map/ppermute | solution.py:255
  2.0 0.8 %edges.1 = f32[4,4,128]{2,1,0:T(4,128)S(1)} custom-call(f32[1008,128]{1,0:T(8,128)S(1)} %get-tuple-element.12.refs_0_), custom_call_target="tpu_custom_call" | custom-call | tf_op jit(solution)/shard_map/edges/pallas_call | solution.py:256
  2.8 0.2 %collective-permute-done.refs_8_ = f32[63,4,128]{2,1,0:T(4,128)S(1)} collective-permute-done((f32[63,4,128]{2,1,0:T(4,128)S(1)}, f32[63,4,128]{2,1,0:T(4,128)S(1)}, u32[]{:S(2)}, u32[]{:S(2)}) %collective-permute-start) | collective-permute-done | bytes 129056 | tf_op jit(solution)/shard_map/ppermute | solution.py:255
  3.0 0.0 copy-start.3
  3.0 3.9 %collective-permute-start.4 = (f32[67,4,128]{2,1,0:T(4,128)S(1)}, f32[67,4,128]{2,1,0:T(4,128)S(1)}, u32[]{:S(2)}, u32[]{:S(2)}) collective-permute-start(f32[67,4,128]{2,1,0:T(4,128)S(1)} %pad_maximum_fusion.refs_5_), channel_id=1, source_target_pairs={{0,12},{4,8},{8,4},{12,0},{1,13},{5,9},{9,5},{13,1},{2,14},{6,10},... | collective-permute-start | bytes 411656 | tf_op jit(solution)/shard_map/ppermute | solution.py:269
  6.9 0.5 %collective-permute-start.3 = (f32[67,4,128]{2,1,0:T(4,128)S(1)}, f32[67,4,128]{2,1,0:T(4,128)S(1)}, u32[]{:S(2)}, u32[]{:S(2)}) collective-permute-start(f32[67,4,128]{2,1,0:T(4,128)S(1)} %pad_maximum_fusion.refs_5_), channel_id=1, source_target_pairs={{0,4},{4,0},{8,12},{12,8},{1,5},{5,1},{9,13},{13,9},{2,6},{6,2},{1... | collective-permute-start | bytes 411656 | tf_op jit(solution)/shard_map/ppermute | solution.py:269
  7.4 0.1 collective-permute-start.5
  7.5 0.0 copy-start.1
  7.5 2.0 %collective-permute-start.1 = (f32[252,128]{1,0:T(8,128)S(1)}, f32[252,128]{1,0:T(8,128)S(1)}, u32[]{:S(2)}, u32[]{:S(2)}) collective-permute-start(f32[252,128]{1,0:T(8,128)S(1)} %get-tuple-element.17), channel_id=1, source_target_pairs={{0,1},{1,0},{2,3},{3,2},{16,17},{17,16},{18,19},{19,18},{4,5},{5,4... | collective-permute-start | bytes 387080 | tf_op jit(solution)/shard_map/ppermute | solution.py:265
  9.5 0.0 collective-permute-start.2
  10.2 0.0 copy-done.3
  10.2 0.0 copy-start.2
  10.2 0.0 copy-done.1
  10.2 0.6 %copy-done.2 = s32[9]{0:T(128)S(1)} copy-done((s32[9]{0:T(128)S(1)}, s32[9]{0:T(128)}, u32[]{:S(2)}) %copy-start.2) | copy-done | bytes 60
  10.9 1.8 %inner.1 = (f32[1008,128]{1,0:T(8,128)S(1)}, f32[13,8,128]{2,1,0:T(8,128)S(1)}, s32[27]{0:T(128)S(4)}) custom-call(f32[1008,128]{1,0:T(8,128)S(1)} %get-tuple-element.12.refs_0_, f32[16,128]{1,0:T(8,128)S(1)} %bitcast.7, f32[7,7]{1,0:T(8,128)S(1)} %bitcast.9, f32[1]{0:T(128)S(6)} %copy.9.refs_3_, s32[9]{0:T(128)S(1)} %copy-done.2, ...), custom_call_target="tpu_custom_call" | custom-call | flops 6451200 | bytes 1032192 | tf_op jit(solution)/shard_map/inner/pallas_call | solution.py:279
  12.7 0.0 collective-permute-done.4.refs_11_
  12.7 1.4 %collective-permute-done.3.refs_9_ = f32[67,4,128]{2,1,0:T(4,128)S(1)} collective-permute-done((f32[67,4,128]{2,1,0:T(4,128)S(1)}, f32[67,4,128]{2,1,0:T(4,128)S(1)}, u32[]{:S(2)}, u32[]{:S(2)}) %collective-permute-start.3) | collective-permute-done | bytes 137248 | tf_op jit(solution)/shard_map/ppermute | solution.py:269
  14.1 0.0 collective-permute-done.1.refs_4_
  14.1 0.0 collective-permute-done.2.refs_5_
  14.1 0.0 collective-permute-done.5.refs_10_
  14.1 1.8 %outer.1 = f32[1008,128]{1,0:T(8,128)} custom-call(f32[1008,128]{1,0:T(8,128)S(1)} %get-tuple-element.14.refs_0_, f32[13,8,128]{2,1,0:T(8,128)S(1)} %get-tuple-element.15.refs_1_, s32[27]{0:T(128)S(4)} %get-tuple-element.16.refs_2_, f32[16,128]{1,0:T(8,128)S(1)} %bitcast.8, f32[252,128]{1,0:T(8,128)S(1)} %collective-permute-done.1.refs_4_, ...), custom_call_target="tpu_custom_call" | custom-call | tf_op jit(solution)/shard_map/outer/pallas_call | solution.py:294
  (4 shorter events, 0.0 us)
Async XLA Ops:
  0.0 1.0 %copy-start = (f32[1,9,7,4,4,128]{5,4,3,2,1,0:T(4,128)S(1)}, f32[1,9,7,4,4,128]{5,4,3,2,1,0:T(4,128)}, u32[]{:S(2)}) copy-start(f32[1,9,7,4,4,128]{5,4,3,2,1,0:T(4,128)} %param.5) | copy-start | bytes 1548292
  1.5 1.5 %collective-permute-start = (f32[63,4,128]{2,1,0:T(4,128)S(1)}, f32[63,4,128]{2,1,0:T(4,128)S(1)}, u32[]{:S(2)}, u32[]{:S(2)}) collective-permute-start(f32[63,4,128]{2,1,0:T(4,128)S(1)} %get-tuple-element.13), channel_id=1, source_target_pairs={{0,16},{16,0},{1,17},{17,1},{2,18},{18,2},{3,19},{19,3},{4,20},{20... | collective-permute-start | bytes 387080 | tf_op jit(solution)/shard_map/ppermute | solution.py:255
  3.0 7.2 %copy-start.3 = (f32[1,7,7]{2,0,1:T(1,128)S(1)}, f32[1,7,7]{2,0,1:T(1,128)}, u32[]{:S(2)}) copy-start(f32[1,7,7]{2,0,1:T(1,128)} %param.7) | copy-start | bytes 592
  3.0 9.7 %collective-permute-start.4 = (f32[67,4,128]{2,1,0:T(4,128)S(1)}, f32[67,4,128]{2,1,0:T(4,128)S(1)}, u32[]{:S(2)}, u32[]{:S(2)}) collective-permute-start(f32[67,4,128]{2,1,0:T(4,128)S(1)} %pad_maximum_fusion.refs_5_), channel_id=1, source_target_pairs={{0,12},{4,8},{8,4},{12,0},{1,13},{5,9},{9,5},{13,1},{2,14},{6,10},... | collective-permute-start | bytes 411656 | tf_op jit(solution)/shard_map/ppermute | solution.py:269
  6.9 7.2 %collective-permute-start.3 = (f32[67,4,128]{2,1,0:T(4,128)S(1)}, f32[67,4,128]{2,1,0:T(4,128)S(1)}, u32[]{:S(2)}, u32[]{:S(2)}) collective-permute-start(f32[67,4,128]{2,1,0:T(4,128)S(1)} %pad_maximum_fusion.refs_5_), channel_id=1, source_target_pairs={{0,4},{4,0},{8,12},{12,8},{1,5},{5,1},{9,13},{13,9},{2,6},{6,2},{1... | collective-permute-start | bytes 411656 | tf_op jit(solution)/shard_map/ppermute | solution.py:269
  7.4 6.6 %collective-permute-start.5 = (f32[67,4,128]{2,1,0:T(4,128)S(1)}, f32[67,4,128]{2,1,0:T(4,128)S(1)}, u32[]{:S(2)}, u32[]{:S(2)}) collective-permute-start(f32[67,4,128]{2,1,0:T(4,128)S(1)} %pad_maximum_fusion.refs_5_), channel_id=1, source_target_pairs={{0,8},{4,12},{8,0},{12,4},{1,9},{5,13},{9,1},{13,5},{2,10},{6,14},... | collective-permute-start | bytes 411656 | tf_op jit(solution)/shard_map/ppermute | solution.py:269
  7.5 2.7 %copy-start.1 = (f32[1,4,4,128]{3,2,1,0:T(4,128)S(1)}, f32[1,4,4,128]{3,2,1,0:T(4,128)}, u32[]{:S(2)}) copy-start(f32[1,4,4,128]{3,2,1,0:T(4,128)} %param.6) | copy-start | bytes 24580
  7.5 6.5 %collective-permute-start.1 = (f32[252,128]{1,0:T(8,128)S(1)}, f32[252,128]{1,0:T(8,128)S(1)}, u32[]{:S(2)}, u32[]{:S(2)}) collective-permute-start(f32[252,128]{1,0:T(8,128)S(1)} %get-tuple-element.17), channel_id=1, source_target_pairs={{0,1},{1,0},{2,3},{3,2},{16,17},{17,16},{18,19},{19,18},{4,5},{5,4... | collective-permute-start | bytes 387080 | tf_op jit(solution)/shard_map/ppermute | solution.py:265
  9.5 4.6 %collective-permute-start.2 = (f32[252,128]{1,0:T(8,128)S(1)}, f32[252,128]{1,0:T(8,128)S(1)}, u32[]{:S(2)}, u32[]{:S(2)}) collective-permute-start(f32[252,128]{1,0:T(8,128)S(1)} %get-tuple-element.18), channel_id=1, source_target_pairs={{0,16},{1,2},{2,1},{3,19},{16,0},{17,18},{18,17},{19,3},{4,20},{5,... | collective-permute-start | bytes 387080 | tf_op jit(solution)/shard_map/ppermute | solution.py:266
  10.2 0.7 %copy-start.2 = (s32[9]{0:T(128)S(1)}, s32[9]{0:T(128)}, u32[]{:S(2)}) copy-start(s32[9]{0:T(128)} %refs_4_.1) | copy-start | bytes 112

commit v3 on v2

--- a/solution.py
+++ b/solution.py
@@ -33,36 +33,73 @@
     return route
 
 
-def collect_kernel(tiles, source_ref, state_ref, strip_ref, even_ref, odd_ref, sem):
-    copy = pltpu.make_async_copy(source_ref, state_ref, sem)
-    copy.start()
+def collect_kernel(
+    times,
+    fields,
+    source_ref,
+    offset_source_ref,
+    state_ref,
+    edge_ref,
+    even_ref,
+    odd_ref,
+    place_ref,
+    offset_ref,
+    sems,
+    offset_sem,
+):
+    block_rows = fields * 16
+    plan = pltpu.make_async_copy(offset_source_ref, offset_ref, offset_sem)
+
+    def piece(t):
+        rows = pl.ds(t * block_rows, block_rows)
+        return pltpu.make_async_copy(source_ref.at[rows, :], state_ref.at[rows, :], sems.at[t])
+
+    for t in range(times):
+        piece(t).start()
+    plan.start()
+    lane = lax.broadcasted_iota(jnp.int32, (16, 128), 1)
+    edge = jnp.zeros((16, 128), jnp.float32)
+    for t in range(times):
+        piece(t).wait()
+        for f in range(fields):
+            i = t * fields + f
+            block = state_ref[pl.ds(16 * i, 16), :]
+            here = jnp.logical_or(lane == 2 * i, lane == 2 * i + 1)
+            edge = jnp.where(here, pltpu.roll(block, 2 * i + 1, 1), edge)
+    for a in range(4):
+        edge_ref[a] = edge[4 * a : 4 * a + 4]
+
     slab, slabs = lax.axis_index("span"), lax.axis_size("span")
     parity = lax.rem(slab, 2)
     paired_even = (slab ^ 1) < slabs
     paired_odd = jnp.logical_and(slab > 0, ((slab - 1) ^ 1) + 1 < slabs)
-    copy.wait()
-    low = state_ref[pl.ds(0, 4 * tiles, stride=4), :]
-    high = state_ref[pl.ds(3, 4 * tiles, stride=4), :]
+    low = state_ref[pl.ds(0, 4 * times * fields, stride=4), :]
+    high = state_ref[pl.ds(3, 4 * times * fields, stride=4), :]
     even_ref[...] = jnp.where(paired_even, jnp.where(parity == 0, high, low), 0.0)
     odd_ref[...] = jnp.where(paired_odd, jnp.where(parity == 0, low, high), 0.0)
 
-    def step(i, _):
-        strip_ref[i] = state_ref[pl.ds(i * 16 + 12, 4), :]
-        return 0
-
-    lax.fori_loop(0, tiles, step, 0, unroll=9)
-
-
-def edge_kernel(tiles, state_ref, edge_ref):
-    lane = lax.broadcasted_iota(jnp.int32, (16, 128), 1)
-
-    def step(i, edge):
-        block = state_ref[pl.ds(pl.multiple_of(i * 16, 16), 16), :]
-        return jnp.where(lane // 2 == i, pltpu.roll(block, 2 * i + 1, 1), edge)
-
-    edge = lax.fori_loop(0, tiles, step, jnp.zeros((16, 128), jnp.float32), unroll=7)
+    plan.wait()
+    sectors = lax.axis_size("sec")
+    row, sec = lax.axis_index("row"), lax.axis_index("sec")
+    total = sectors * 128
+    for t in range(times):
+        offset = offset_ref[t]
+        shift = jnp.where(row == 0, offset, lax.rem(total - offset, total))
+        whole = shift // 128
+        near = lax.rem(sec - whole + sectors, sectors)
+        far = lax.rem(sec - whole - 1 + 2 * sectors, sectors)
+        if sectors == 4:
+            near, far = near ^ sec, far ^ sec
+        place_ref[3 * t] = near
+        place_ref[3 * t + 1] = far
+        place_ref[3 * t + 2] = shift - 128 * whole
+
+
+def pack_kernel(tiles, swapped_ref, edge_ref, packed_ref):
+    for i in range(tiles):
+        packed_ref[i] = swapped_ref[pl.ds(16 * i + 12, 4), :]
     for a in range(4):
-        edge_ref[a] = edge[4 * a : 4 * a + 4]
+        packed_ref[tiles + a] = edge_ref[a]
 
 
 def inner_kernel(
@@ -72,14 +109,10 @@
     coeff_ref,
     jac_ref,
     omega_ref,
-    offset_ref,
     _,
     partial_ref,
     mix_ref,
-    place_ref,
 ):
-    sectors = lax.axis_size("sec")
-    row, sec = lax.axis_index("row"), lax.axis_index("sec")
     lane = lax.broadcasted_iota(jnp.int32, (8, 128), 1)
     sub = lax.broadcasted_iota(jnp.int32, (8, 128), 0)
     lower = sub < 4
@@ -100,18 +133,6 @@
         mix_ref[fields - 1 + distance] = sign * mix
 
     def step(t, _):
-        offset = offset_ref[t]
-        total = sectors * 128
-        shift = jnp.where(row == 0, offset, lax.rem(total - offset, total))
-        whole = shift // 128
-        near = lax.rem(sec - whole + sectors, sectors)
-        far = lax.rem(sec - whole - 1 + 2 * sectors, sectors)
-        if sectors == 4:
-            near, far = near ^ sec, far ^ sec
-        place_ref[3 * t] = near
-        place_ref[3 * t + 1] = far
-        place_ref[3 * t + 2] = shift - 128 * whole
-
         def load(u, f, h):
             start = pl.multiple_of((u * fields + f) * 16 + 8 * h, 8)
             return state_ref[pl.ds(start, 8), :]
@@ -238,30 +259,37 @@
     flat = state.reshape(tiles * 16, cells)
     coeff = viscosity.reshape(16, cells)
     f32 = jnp.float32
-    local, strip, even, odd = pl.pallas_call(
-        lambda *refs: collect_kernel(tiles, *refs),
+    swapped = lax.ppermute(flat, "row", [(0, 1), (1, 0)])
+    local, edge, even, odd, place = pl.pallas_call(
+        lambda *refs: collect_kernel(times, fields, *refs),
         out_shape=[
             pltpu.VMEM((tiles * 16, cells), f32),
-            pltpu.VMEM((tiles, 4, cells), f32),
+            pltpu.VMEM((4, 4, cells), f32),
             pltpu.VMEM((tiles * 4, cells), f32),
             pltpu.VMEM((tiles * 4, cells), f32),
+            pltpu.SMEM((3 * times,), jnp.int32),
         ],
-        in_specs=[ANY],
-        out_specs=[VMEM] * 4,
-        scratch_shapes=[pltpu.SemaphoreType.DMA],
+        in_specs=[ANY, ANY],
+        out_specs=[VMEM] * 4 + [SMEM],
+        scratch_shapes=[
+            pltpu.SMEM((times,), jnp.int32),
+            pltpu.SemaphoreType.DMA((times,)),
+            pltpu.SemaphoreType.DMA,
+        ],
         compiler_params=LIMIT,
         name="collect",
-    )(flat)
-    swapped = lax.ppermute(strip, "row", [(0, 1), (1, 0)])
-    edge = pl.pallas_call(
-        lambda *refs: edge_kernel(tiles, *refs),
-        out_shape=pltpu.VMEM((4, 4, cells), f32),
-        in_specs=[VMEM],
+    )(
+        pltpu.with_memory_space_constraint(flat, pltpu.HBM),
+        pltpu.with_memory_space_constraint(offsets, pltpu.HBM),
+    )
+    packed = pl.pallas_call(
+        lambda *refs: pack_kernel(tiles, *refs),
+        out_shape=pltpu.VMEM((tiles + 4, 4, cells), f32),
+        in_specs=[VMEM, VMEM],
         out_specs=VMEM,
         compiler_params=LIMIT,
-        name="edges",
-    )(local)
-    packed = jnp.concatenate([swapped, edge], axis=0)
+        name="pack",
+    )(swapped, edge)
     even = lax.ppermute(even, ("row", "span"), slab_pairs(slabs, 0))
     odd = lax.ppermute(odd, ("row", "span"), slab_pairs(slabs, 1))
     if sectors == 4:
@@ -269,28 +297,26 @@
             lax.ppermute(packed, "sec", [(k, k ^ distance) for k in range(sectors)])
             for distance in (1, 2, 3)
         ]
-        sources = [swapped] + near
-        edge_a = edge_b = None
+        sources = [packed] + near
         edge_a, edge_b = near[0][tiles:], near[2][tiles:]
     else:
-        sources = [lax.all_gather(swapped, "sec")]
+        sources = [lax.all_gather(packed[:tiles], "sec")]
         edge_a = lax.ppermute(edge, "sec", sector_pairs(sectors, 0))
         edge_b = lax.ppermute(edge, "sec", sector_pairs(sectors, 1))
-    partial, mix, place = pl.pallas_call(
+    partial, mix = pl.pallas_call(
         lambda *refs: inner_kernel(times, fields, *refs),
         out_shape=[
             pltpu.VMEM((tiles * 16, cells), f32),
             pltpu.VMEM((2 * fields - 1, 8, cells), f32),
-            pltpu.SMEM((3 * times,), jnp.int32),
         ],
-        in_specs=[VMEM, VMEM, SMEM, SMEM, SMEM, ANY],
-        out_specs=[VMEM, VMEM, SMEM],
+        in_specs=[VMEM, VMEM, SMEM, SMEM, ANY],
+        out_specs=[VMEM, VMEM],
         compiler_params=LIMIT,
         cost_estimate=pl.CostEstimate(
             flops=tiles * 16 * cells * 50, bytes_accessed=tiles * 16 * cells * 8, transcendentals=0
         ),
         name="inner",
-    )(local, coeff, jacobian[0], frequency, offsets, packed)
+    )(local, coeff, jacobian[0], frequency, packed)
     out = pl.pallas_call(
         lambda *refs: outer_kernel(times, fields, sectors, *refs),
         out_shape=jax.ShapeDtypeStruct(flat.shape, f32),

time: 16.1 us -> 15.4 us (0.957)
  local copies, waits for them, and re-layouts: 1.7 us -> 0.02 us
  Pallas kernels: 4.84 us -> 5.43 us
  waiting for transfers between devices: 1.59 us -> 2.13 us
    unnamed x9 -> x5, local copies, waits for them, and re-layouts: 1.69 us -> 0.02 us
    ppermute x3, waiting for transfers between devices: 1.36 us -> 2.13 us  [on_device(): lax.ppermute(packed, 'sec', [(k, k ^ distance) for k in range(sectors)])]
    pallas_call x2, Pallas kernels: 1.19 us -> 1.82 us  [the longest x1 1.79 us: on_device(): pl.pallas_call(lambda *refs: collect_kernel(times, fields, *refs), out_sh...]
    ppermute x1, waiting for transfers between devices: 0.22 us -> 0.01 us  [on_device(): swapped = lax.ppermute(flat, 'row', [(0, 1), (1, 0)])]
  transfers between devices with their start and end apart: 6 -> 6, of which waited for: 2 -> 1; matrix products, arithmetic and copies ran while one was open for 0% -> 0% of each run, Pallas kernels for 16% -> 23%
where the time goes in v3:
time: 15.4 us; the launch traced here: 15.2 us
  starting transfers between devices  6.87 us (45%)
  Pallas kernels  5.43 us (35%)
  waiting for transfers between devices  2.13 us (14%)
  between operations  0.75 us (5%)
    ppermute x3, starting transfers between devices, on_device(): lax.ppermute(packed, 'sec', [(k, k ^ distance) for k in range(sectors)])  4.44 us
    ppermute x3, waiting for transfers between devices, on_device(): lax.ppermute(packed, 'sec', [(k, k ^ distance) for k in range(sectors)])  2.13 us
    ppermute x1, starting transfers between devices, on_device(): even = lax.ppermute(even, ('row', 'span'), slab_pairs(slabs, 0))  1.98 us
    pallas_call x1, Pallas kernels, on_device(): pl.pallas_call(lambda *refs: outer_kernel(times, fields, sectors, *refs),...  1.84 us
    pallas_call x1, Pallas kernels, on_device(): pl.pallas_call(lambda *refs: collect_kernel(times, fields, *refs), out_sh...  1.79 us
    pallas_call x1, Pallas kernels, on_device(): pl.pallas_call(lambda *refs: inner_kernel(times, fields, *refs), out_shap...  1.78 us
    ppermute x1, starting transfers between devices, on_device(): swapped = lax.ppermute(flat, 'row', [(0, 1), (1, 0)])  0.45 us
  transfers between devices with their start and end apart: 6, of which 1 were waited for; matrix products, arithmetic and copies ran while one was open for 0% of the time, Pallas kernels for 23%

profile of v3, /device:TPU:0, one launch (start us, length us, event | category | flops | bytes accessed | tf_op | source)
XLA Modules:
  0.0 15.2 jit_solution(18356749368786378400)
XLA Ops:
  0.0 0.5 %collective-permute-start = (f32[1008,128]{1,0:T(8,128)}, f32[1008,128]{1,0:T(8,128)S(1)}, u32[]{:S(2)}, u32[]{:S(2)}) collective-permute-start(f32[1008,128]{1,0:T(8,128)} %bitcast.9), channel_id=1, source_target_pairs={{0,16},{16,0},{1,17},{17,1},{2,18},{18,2},{3,19},{19,3},{4,20},{20... | collective-permute-start | bytes 1548296 | tf_op jit(solution)/shard_map/ppermute | solution.py:262
  0.5 1.8 %collect.1 = (f32[1008,128]{1,0:T(8,128)S(1)}, f32[4,4,128]{2,1,0:T(4,128)S(1)}, f32[252,128]{1,0:T(8,128)S(1)}, f32[252,128]{1,0:T(8,128)S(1)}, s32[27]{0:T(128)S(4)}) custom-call(f32[1008,128]{1,0:T(8,128)} %bitcast.10, s32[9]{0:T(128)} %refs_1_.1), custom_call_target="tpu_custom_call" | custom-call | tf_op jit(solution)/shard_map/collect/pallas_call | solution.py:263
  2.3 0.0 collective-permute-done.refs_0_
  2.3 0.0 copy-start.1
  2.3 3.8 %collective-permute-start.4 = (f32[67,4,128]{2,1,0:T(4,128)S(1)}, f32[67,4,128]{2,1,0:T(4,128)S(1)}, u32[]{:S(2)}, u32[]{:S(2)}) collective-permute-start(f32[67,4,128]{2,1,0:T(4,128)S(1)} %pack.1.refs_4_.refs_8_), channel_id=1, source_target_pairs={{0,12},{4,8},{8,4},{12,0},{1,13},{5,9},{9,5},{13,1},{2,14},{6,10},... | collective-permute-start | bytes 411656 | tf_op jit(solution)/shard_map/ppermute | solution.py:297
  6.1 0.5 %collective-permute-start.3 = (f32[67,4,128]{2,1,0:T(4,128)S(1)}, f32[67,4,128]{2,1,0:T(4,128)S(1)}, u32[]{:S(2)}, u32[]{:S(2)}) collective-permute-start(f32[67,4,128]{2,1,0:T(4,128)S(1)} %pack.1.refs_4_.refs_8_), channel_id=1, source_target_pairs={{0,4},{4,0},{8,12},{12,8},{1,5},{5,1},{9,13},{13,9},{2,6},{6,2},{1... | collective-permute-start | bytes 411656 | tf_op jit(solution)/shard_map/ppermute | solution.py:297
  6.6 0.1 collective-permute-start.5
  6.8 2.0 %collective-permute-start.1 = (f32[252,128]{1,0:T(8,128)S(1)}, f32[252,128]{1,0:T(8,128)S(1)}, u32[]{:S(2)}, u32[]{:S(2)}) collective-permute-start(f32[252,128]{1,0:T(8,128)S(1)} %get-tuple-element.17), channel_id=1, source_target_pairs={{0,1},{1,0},{2,3},{3,2},{16,17},{17,16},{18,19},{19,18},{4,5},{5,4... | collective-permute-start | bytes 387080 | tf_op jit(solution)/shard_map/ppermute | solution.py:293
  8.7 0.0 copy-start
  8.7 0.0 collective-permute-start.2
  9.4 0.0 copy-done.1
  9.4 0.0 copy-done
  9.4 1.8 %inner.1 = (f32[1008,128]{1,0:T(8,128)S(1)}, f32[13,8,128]{2,1,0:T(8,128)S(1)}) custom-call(f32[1008,128]{1,0:T(8,128)S(1)} %get-tuple-element.12.refs_0_, f32[16,128]{1,0:T(8,128)S(1)} %bitcast.6, f32[7,7]{1,0:T(8,128)S(1)} %bitcast.8, f32[1]{0:T(128)S(6)} %copy.9.refs_3_, f32[67,4,128]{2,1,0:T(4,128)S(1)} %pack.1.refs_4_.refs_8_), custom_call_target="tpu_custom_call" | custom-call | flops 6451200 | bytes 1032192 | tf_op jit(solution)/shard_map/inner/pallas_call | solution.py:306
  11.2 0.0 collective-permute-done.4.refs_11_
  11.2 2.1 %collective-permute-done.3.refs_9_ = f32[67,4,128]{2,1,0:T(4,128)S(1)} collective-permute-done((f32[67,4,128]{2,1,0:T(4,128)S(1)}, f32[67,4,128]{2,1,0:T(4,128)S(1)}, u32[]{:S(2)}, u32[]{:S(2)}) %collective-permute-start.3) | collective-permute-done | bytes 137248 | tf_op jit(solution)/shard_map/ppermute | solution.py:297
  13.3 0.0 collective-permute-done.1.refs_4_
  13.4 0.0 collective-permute-done.2.refs_5_
  13.4 0.0 collective-permute-done.5.refs_10_
  13.4 1.8 %outer.1 = f32[1008,128]{1,0:T(8,128)} custom-call(f32[1008,128]{1,0:T(8,128)S(1)} %get-tuple-element.14.refs_0_, f32[13,8,128]{2,1,0:T(8,128)S(1)} %get-tuple-element.15.refs_1_, s32[27]{0:T(128)S(4)} %get-tuple-element.16.refs_2_, f32[16,128]{1,0:T(8,128)S(1)} %bitcast.7, f32[252,128]{1,0:T(8,128)S(1)} %collective-permute-done.1.refs_4_, ...), custom_call_target="tpu_custom_call" | custom-call | tf_op jit(solution)/shard_map/outer/pallas_call | solution.py:320
  (4 shorter events, 0.0 us)
Async XLA Ops:
  0.0 2.3 %collective-permute-start = (f32[1008,128]{1,0:T(8,128)}, f32[1008,128]{1,0:T(8,128)S(1)}, u32[]{:S(2)}, u32[]{:S(2)}) collective-permute-start(f32[1008,128]{1,0:T(8,128)} %bitcast.9), channel_id=1, source_target_pairs={{0,16},{16,0},{1,17},{17,1},{2,18},{18,2},{3,19},{19,3},{4,20},{20... | collective-permute-start | bytes 1548296 | tf_op jit(solution)/shard_map/ppermute | solution.py:262
  2.3 7.1 %copy-start.1 = (f32[1,7,7]{2,0,1:T(1,128)S(1)}, f32[1,7,7]{2,0,1:T(1,128)}, u32[]{:S(2)}) copy-start(f32[1,7,7]{2,0,1:T(1,128)} %param.7) | copy-start | bytes 592
  2.3 8.9 %collective-permute-start.4 = (f32[67,4,128]{2,1,0:T(4,128)S(1)}, f32[67,4,128]{2,1,0:T(4,128)S(1)}, u32[]{:S(2)}, u32[]{:S(2)}) collective-permute-start(f32[67,4,128]{2,1,0:T(4,128)S(1)} %pack.1.refs_4_.refs_8_), channel_id=1, source_target_pairs={{0,12},{4,8},{8,4},{12,0},{1,13},{5,9},{9,5},{13,1},{2,14},{6,10},... | collective-permute-start | bytes 411656 | tf_op jit(solution)/shard_map/ppermute | solution.py:297
  6.1 7.2 %collective-permute-start.3 = (f32[67,4,128]{2,1,0:T(4,128)S(1)}, f32[67,4,128]{2,1,0:T(4,128)S(1)}, u32[]{:S(2)}, u32[]{:S(2)}) collective-permute-start(f32[67,4,128]{2,1,0:T(4,128)S(1)} %pack.1.refs_4_.refs_8_), channel_id=1, source_target_pairs={{0,4},{4,0},{8,12},{12,8},{1,5},{5,1},{9,13},{13,9},{2,6},{6,2},{1... | collective-permute-start | bytes 411656 | tf_op jit(solution)/shard_map/ppermute | solution.py:297
  6.6 6.7 %collective-permute-start.5 = (f32[67,4,128]{2,1,0:T(4,128)S(1)}, f32[67,4,128]{2,1,0:T(4,128)S(1)}, u32[]{:S(2)}, u32[]{:S(2)}) collective-permute-start(f32[67,4,128]{2,1,0:T(4,128)S(1)} %pack.1.refs_4_.refs_8_), channel_id=1, source_target_pairs={{0,8},{4,12},{8,0},{12,4},{1,9},{5,13},{9,1},{13,5},{2,10},{6,14},... | collective-permute-start | bytes 411656 | tf_op jit(solution)/shard_map/ppermute | solution.py:297
  6.8 6.6 %collective-permute-start.1 = (f32[252,128]{1,0:T(8,128)S(1)}, f32[252,128]{1,0:T(8,128)S(1)}, u32[]{:S(2)}, u32[]{:S(2)}) collective-permute-start(f32[252,128]{1,0:T(8,128)S(1)} %get-tuple-element.17), channel_id=1, source_target_pairs={{0,1},{1,0},{2,3},{3,2},{16,17},{17,16},{18,19},{19,18},{4,5},{5,4... | collective-permute-start | bytes 387080 | tf_op jit(solution)/shard_map/ppermute | solution.py:293
  8.7 0.7 %copy-start = (f32[1,4,4,128]{3,2,1,0:T(4,128)S(1)}, f32[1,4,4,128]{3,2,1,0:T(4,128)}, u32[]{:S(2)}) copy-start(f32[1,4,4,128]{3,2,1,0:T(4,128)} %param.6) | copy-start | bytes 24580
  8.7 4.6 %collective-permute-start.2 = (f32[252,128]{1,0:T(8,128)S(1)}, f32[252,128]{1,0:T(8,128)S(1)}, u32[]{:S(2)}, u32[]{:S(2)}) collective-permute-start(f32[252,128]{1,0:T(8,128)S(1)} %get-tuple-element.18), channel_id=1, source_target_pairs={{0,16},{1,2},{2,1},{3,19},{16,0},{17,18},{18,17},{19,3},{4,20},{5,... | collective-permute-start | bytes 387080 | tf_op jit(solution)/shard_map/ppermute | solution.py:294
